TPU v7x, 512 devices: a whole 4x8x8 slice. The times are simulated.
512 devices in a mesh: sib: 2 (over core), row: 16 (over z, y_lo), col: 16 (over x, y_hi).
Axes of the slice: x: 4, y: 8 (y_hi: 4, y_lo: 2; y = y_hi * 2 + y_lo), z: 8, core: 2. Of those that a mesh axis runs over, the one named last changes fastest.
Arguments:
- child_front: float32 [2, 8192, 8192], P('sib', 'row', 'col'), may hold values from -6 to 6
- child_panel: float32 [2, 8192, 1024], P('sib', ('row', 'col')), may hold values from -0.42 to 0.42
- block_map: int32 [2, 64], replicated, may hold values from 0 to 95, as said below
- parent_front: float32 [12288, 12288], P(('row', 'sib'), 'col'), may hold values from -6 to 6
- pivot_inverse: float32 [512, 512], replicated, may hold values from -0.03 to 0.1, as said below
Outputs:
- parent_out: float32 [12288, 12288], P(('row', 'sib'), 'col')
Inputs may be any that keep to these rules, and one draw needn't show every extreme that they name: `block_map`: each row is strictly increasing. A child block i that lands in parent block g * 6 + k with 0 <= k < 6 satisfies g * 4 - 2 <= i < (g + 1) * 4; the lower end is met for g = 1 in every draw, and the last parent block is always named. `pivot_inverse`: lower triangular with diagonal entries from 0.05 to 0.1.
All inputs are finite; a program needn't handle non-finite values.
Results may differ from a plain program's by a relative error of at most 0.0001.
Values sent between devices are 32-bit elements; how exact they have to be, the bound alone decides.
A program may use at most 64 MiB of HBM per device.

v0:
```python
import jax
import jax.numpy as jnp
from jax import lax
from jax.sharding import Mesh
from jax.sharding import PartitionSpec as P

BLK = 128
CBD = 4
PBD = 6
HB = 2
PANEL = 512
ROW = ("row_0", "row_1")
ROW_COL = ("row_0", "row_1", "col")
ROW_SIB = ("row_0", "row_1", "sib")


def broadcast_by_axis(value, axes, root):
    value = jnp.where(lax.axis_index(axes) == root, value, jnp.zeros_like(value))
    for axis in axes:
        value = lax.psum(value, axis)
    return value


def shifted(value, axis, steps):
    count = lax.axis_size(axis)
    initial, last = (max(0, -steps), min(count, count - steps))
    return lax.ppermute(value, axis, [(source, source + steps) for source in range(initial, last)])


def split_up(value, dim, devices):
    shape = value.shape
    blocks = value.reshape(*shape[:dim], devices, shape[dim] // devices, *shape[dim + 1 :])
    return jnp.moveaxis(blocks, dim, 0)


def summed_on_arrival(value, axis, dim):
    blocks = split_up(value, dim, lax.axis_size(axis))
    arrived = lax.all_to_all(blocks, axis, split_axis=0, concat_axis=0, tiled=True)
    return arrived.sum(axis=0)


def padded_to(lines, devices):
    spare = -len(lines) % devices
    return jnp.pad(lines, [(0, spare)] + [(0, 0)] * (lines.ndim - 1))


def spread(value, axis, root):
    lines = jnp.where(lax.axis_index(axis) == root, value, jnp.zeros_like(value)).reshape(
        -1, *value.shape[1:][-1:]
    )
    padded = padded_to(lines, lax.axis_size(axis))
    own = lax.psum_scatter(padded, axis, scatter_dimension=0, tiled=True)
    return lax.all_gather(own, axis, axis=0, tiled=True)[: len(lines)].reshape(value.shape)


def from_everyone(value, axis):
    devices = lax.axis_size(axis)
    return lax.all_to_all(
        jnp.broadcast_to(value[None], (devices, *value.shape)), axis, 0, 0, tiled=True
    )


def joined_along(blocks, dim):
    shape = list(blocks.shape[1:])
    shape[dim] *= blocks.shape[0]
    return jnp.moveaxis(blocks, 0, dim).reshape(shape)


def collect(value, axis, dim):
    blocks = from_everyone(value, axis)
    return joined_along(blocks, dim)


def choose_blocks(block_row, device, child_span, parent_span, edge_span):
    padded = jnp.concatenate([jnp.full((edge_span,), -1, jnp.int32), block_row])
    window = lax.dynamic_slice_in_dim(padded, device * child_span, child_span + edge_span)
    target = device * parent_span + jnp.arange(parent_span, dtype=jnp.int32)
    return (window[None, :] == target[:, None]).astype(jnp.float32)


def times_inverse(rows_part, pivot_inverse):
    return lax.dot_general(
        rows_part,
        pivot_inverse,
        (((1,), (1,)), ((), ())),
        precision=lax.Precision.HIGHEST,
        preferred_element_type=jnp.float32,
    )


def shards(child_front, child_panel, block_map, parent_front, pivot_inverse):
    front_index = lax.axis_index("sib")
    row_index = lax.axis_index(ROW)
    col_index = lax.axis_index("col")
    child_rows = child_front.shape[1]
    parent_rows = parent_front.shape[0]
    parent_cols = parent_front.shape[1]
    edge_width = HB * BLK
    span_blocks = CBD + HB
    rows_local = lax.all_gather(child_panel, "col", axis=1, tiled=True)[0]
    cols_local = broadcast_by_axis(rows_local, ROW, col_index)
    update = child_front[0] - lax.dot_general(
        rows_local,
        cols_local,
        (((1,), (1,)), ((), ())),
        precision=lax.Precision.HIGHEST,
        preferred_element_type=jnp.float32,
    )
    my_map = lax.dynamic_index_in_dim(block_map, front_index, 0, keepdims=False)
    left_cols = shifted(update[:, -edge_width:], "col", 1)
    col_window = jnp.concatenate([left_cols, update], axis=1).reshape(child_rows, span_blocks, BLK)
    col_pick = choose_blocks(my_map, col_index, CBD, PBD, HB)
    spread_cols = jnp.einsum(
        "rwk,qw->rqk", col_window, col_pick, precision=lax.Precision.HIGHEST
    ).reshape(child_rows, PBD * BLK)
    left_rows = shifted(spread_cols[-edge_width:], ROW, 1)
    row_window = jnp.concatenate([left_rows, spread_cols], axis=0).reshape(
        span_blocks, BLK, PBD * BLK
    )
    row_pick = choose_blocks(my_map, row_index, CBD, PBD, HB)
    spread_both = jnp.einsum(
        "wtc,qw->qtc", row_window, row_pick, precision=lax.Precision.HIGHEST
    ).reshape(PBD * BLK, PBD * BLK)
    summed = summed_on_arrival(spread_both, "sib", 0)
    assembled = parent_front + summed
    local_factor = times_inverse(assembled[:, :PANEL], pivot_inverse)
    factor_rows = spread(local_factor, "col", 0)
    owner_rows = broadcast_by_axis(factor_rows, ROW, col_index)
    col_factor = collect(owner_rows, "sib", 0)
    product = lax.dot_general(
        factor_rows,
        col_factor,
        (((1,), (1,)), ((), ())),
        precision=lax.Precision.HIGHEST,
        preferred_element_type=jnp.float32,
    )
    global_rows = (row_index * 2 + front_index) * parent_rows + jnp.arange(
        parent_rows, dtype=jnp.int32
    )
    global_cols = col_index * parent_cols + jnp.arange(parent_cols, dtype=jnp.int32)
    inside = (global_rows[:, None] >= PANEL) & (global_cols[None, :] >= PANEL)
    trailing = jnp.where(inside, assembled - product, assembled)
    factor_wide = jnp.pad(factor_rows, ((0, 0), (0, parent_cols - PANEL)))
    return jnp.where(global_cols[None, :] < PANEL, factor_wide, trailing)


def solution(mesh):
    split = Mesh(
        mesh.devices.reshape(mesh.shape["sib"], 8, 2, mesh.shape["col"]),
        ("sib", "row_0", "row_1", "col"),
    )
    placed = (P("sib", ROW, "col"), P("sib", ROW_COL, None), P(), P(ROW_SIB, "col"), P())
    return jax.shard_map(
        shards, mesh=split, in_specs=placed, out_specs=P(ROW_SIB, "col"), check_vma=False
    )
```

profile of v0, /device:TPU:1, one launch (start us, length us, event | category | flops | bytes accessed | tf_op | source)
XLA Modules:
  0.0 621.0 jit_solution(6062125449259001521)
XLA Ops:
  6.5 0.0 copy-start
  6.5 0.0 all-gather.2.cloned.1.call-start
  6.5 0.7 all-gather.2.cloned.1.call-update
  7.3 0.0 all-reduce.7.cloned.1.call-start
  7.3 72.9 %all-gather.2.cloned.1.call-done = f32[1,512,1024]{2,1,0:T(8,128)} async-done(((f32[1,32,1024]{2,1,0:T(8,128)}), f32[1,512,1024]{2,1,0:T(8,128)}) %all-gather.2.cloned.1.call-update) | async-done | bytes 2097168 | tf_op jit(solution)/shard_map/all_gather | solution.py:100
  80.2 3.2 bitcast_select_fusion
  83.4 0.0 all-reduce.7.cloned.1.call-update
  83.4 0.0 all-reduce.9.cloned.1.call-start
  83.4 82.9 %all-reduce.7.cloned.1.call-done = f32[512,1024]{1,0:T(8,128)} async-done(((f32[512,1024]{1,0:T(8,128)}), f32[512,1024]{1,0:T(8,128)}) %all-reduce.7.cloned.1.call-update) | async-done | bytes 2097168 | tf_op jit(solution)/shard_map/psum | solution.py:20
  166.4 0.0 all-reduce.9.cloned.1.call-update
  166.4 0.0 reduce-scatter.2.cloned.1.call-start
  166.4 2.7 copy.8
  169.1 81.5 %all-reduce.9.cloned.1.call-done = f32[512,1024]{1,0:T(8,128)} async-done(((f32[512,1024]{1,0:T(8,128)}), f32[512,1024]{1,0:T(8,128)}) %all-reduce.9.cloned.1.call-update) | async-done | bytes 2097168 | tf_op jit(solution)/shard_map/psum | solution.py:20
  250.6 5.4 fusion.8
  256.0 0.0 copy-start.2
  256.0 1.0 copy-done.2
  257.0 4.1 collective-permute-start
  261.1 0.1 pad_dynamic-slice_fusion.1
  261.2 13.7 %collective-permute-done = f32[512,256]{0,1:T(8,128)S(1)} collective-permute-done((f32[512,256]{0,1:T(8,128)S(1)}, f32[512,256]{0,1:T(8,128)S(1)}, u32[]{:S(2)}, u32[]{:S(2)}) %collective-permute-start) | collective-permute-done | bytes 524320 | tf_op jit(solution)/shard_map/ppermute | solution.py:27
  275.0 1.3 pad_maximum_fusion.1
  276.3 1.8 copy.9
  278.2 2.7 convolution_bitcast_fusion
  280.8 1.0 slice.17
  281.9 2.4 copy.10
  284.3 11.1 %collective-permute-start.1 = (f32[256,768]{0,1:T(8,128)}, f32[256,768]{0,1:T(8,128)}, u32[]{:S(2)}, u32[]{:S(2)}) collective-permute-start(f32[256,768]{0,1:T(8,128)} %bitcast.40), channel_id=1, source_target_pairs={{0,16},{16,32},{32,48},{48,64},{64,80},{80,96},{96,112},{112,128},... | collective-permute-start | bytes 2359304 | tf_op jit(solution)/shard_map/ppermute | solution.py:27
  295.4 1.6 copy.11
  297.0 13.2 %collective-permute-done.1 = f32[256,768]{0,1:T(8,128)} collective-permute-done((f32[256,768]{0,1:T(8,128)}, f32[256,768]{0,1:T(8,128)}, u32[]{:S(2)}, u32[]{:S(2)}) %collective-permute-start.1) | collective-permute-done | bytes 786464 | tf_op jit(solution)/shard_map/ppermute | solution.py:27
  310.2 3.2 pad_maximum_fusion
  313.4 2.0 copy.12
  315.4 2.9 fusion
  318.3 0.8 copy.14
  319.1 7.7 %all_to_all.10 = f32[2,384,768]{2,1,0:T(8,128)S(1)} all-to-all(f32[2,384,768]{2,1,0:T(8,128)S(1)} %bitcast.36), channel_id=1, replica_groups=mesh['sib'=2,'row_0'=8,'row_1'=2,'col'=16] {'sib'}, dimensions={0} | all-to-all | bytes 4718592 | tf_op jit(solution)/shard_map/all_to_all | solution.py:38
  326.8 1.3 reduce_sum.9
  328.0 1.8 add.88
  329.8 2.3 convolution_select_fusion
  332.1 0.0 reduce-scatter.2.cloned.1.call-update
  332.2 0.0 all-reduce.11.cloned.1.call-start
  332.2 94.5 %reduce-scatter.2.cloned.1.call-done = f32[24,512]{1,0:T(8,128)} async-done(((f32[384,512]{1,0:T(8,128)}), f32[24,512]{1,0:T(8,128)}) %reduce-scatter.2.cloned.1.call-update) | async-done | bytes 49168 | tf_op jit(solution)/shard_map/reduce_scatter | solution.py:52
  426.7 41.6 %all_gather.7 = f32[384,512]{1,0:T(8,128)S(1)} all-gather(f32[24,512]{1,0:T(8,128)} %reduce-scatter.2.cloned.1.call-done), channel_id=1, replica_groups=mesh['sib'=2,'row_0'=8,'row_1'=2,'col'=16] {'col'}, dimensions={0}, use_global_device_ids=true | all-gather | bytes 835584 | tf_op jit(solution)/shard_map/all_gather | solution.py:53
  468.3 0.9 broadcast_select_fusion
  469.2 0.0 all-reduce.11.cloned.1.call-update
  469.2 0.0 all-reduce.13.cloned.1.call-start
  469.3 78.7 %all-reduce.11.cloned.1.call-done = f32[384,512]{1,0:T(8,128)} async-done(((f32[384,512]{1,0:T(8,128)}), f32[384,512]{1,0:T(8,128)}) %all-reduce.11.cloned.1.call-update) | async-done | bytes 786448 | tf_op jit(solution)/shard_map/psum | solution.py:20
  548.0 0.0 all-reduce.13.cloned.1.call-update
  548.1 56.2 %all-reduce.13.cloned.1.call-done = f32[384,512]{1,0:T(8,128)} async-done(((f32[384,512]{1,0:T(8,128)}), f32[384,512]{1,0:T(8,128)}) %all-reduce.13.cloned.1.call-update) | async-done | bytes 786448 | tf_op jit(solution)/shard_map/psum | solution.py:20
  604.3 1.3 broadcast_in_dim.11
  605.6 5.3 all_to_all.11
  610.9 3.2 fusion.4
  (11 shorter events, 0.1 us)
Async XLA Ops:
  6.5 323.3 %copy-start = (f32[512,512]{1,0:T(8,128)S(1)}, f32[512,512]{1,0:T(8,128)}, u32[]{:S(2)}) copy-start(f32[512,512]{1,0:T(8,128)} %param.9) | copy-start | bytes 3145732
  6.5 73.6 %all-gather.2.cloned.1.call-start = ((), (), s32[]{:S(2)}) async-start(), calls=%async_computation.3 | async-start | bytes 2228224 | tf_op jit(solution)/shard_map/all_gather | solution.py:100
  7.3 159.1 %all-reduce.7.cloned.1.call-start = ((), (), s32[]{:S(2)}) async-start(), calls=%async_computation.4 | async-start | bytes 4194304 | tf_op jit(solution)/shard_map/psum | solution.py:20
  83.4 167.2 %all-reduce.9.cloned.1.call-start = ((), (), s32[]{:S(2)}) async-start(), calls=%async_computation.5 | async-start | bytes 4194304 | tf_op jit(solution)/shard_map/psum | solution.py:20
  166.4 84.2 %copy-start.1 = (f32[1,512,1024]{2,1,0:T(8,128)S(1)}, f32[1,512,1024]{2,1,0:T(8,128)}, u32[]{:S(2)}) copy-start(f32[1,512,1024]{2,1,0:T(8,128)} %all-gather.2.cloned.1.call-done) | copy-start | bytes 6291460
  166.4 260.3 %reduce-scatter.2.cloned.1.call-start = ((), (), s32[]{:S(2)}) async-start(), calls=%async_computation.6 | async-start | bytes 835584 | tf_op jit(solution)/shard_map/reduce_scatter | solution.py:52
  169.1 92.0 %copy-start.3 = (s32[2,64]{1,0:T(2,128)S(1)}, s32[2,64]{1,0:T(2,128)}, u32[]{:S(2)}) copy-start(s32[2,64]{1,0:T(2,128)} %param.7) | copy-start | bytes 1540
  256.0 1.0 copy-start.2
  257.0 17.9 %collective-permute-start = (f32[512,256]{0,1:T(8,128)S(1)}, f32[512,256]{0,1:T(8,128)S(1)}, u32[]{:S(2)}, u32[]{:S(2)}) collective-permute-start(f32[512,256]{0,1:T(8,128)S(1)} %slice.16), channel_id=1, source_target_pairs={{0,1},{1,2},{2,3},{3,4},{4,5},{5,6},{6,7},{7,8},{8,9},{9,10},{10,1... | collective-permute-start | bytes 1572872 | tf_op jit(solution)/shard_map/ppermute | solution.py:27
  284.3 25.9 %collective-permute-start.1 = (f32[256,768]{0,1:T(8,128)}, f32[256,768]{0,1:T(8,128)}, u32[]{:S(2)}, u32[]{:S(2)}) collective-permute-start(f32[256,768]{0,1:T(8,128)} %bitcast.40), channel_id=1, source_target_pairs={{0,16},{16,32},{32,48},{48,64},{64,80},{80,96},{96,112},{112,128},... | collective-permute-start | bytes 2359304 | tf_op jit(solution)/shard_map/ppermute | solution.py:27
  332.2 215.8 %all-reduce.11.cloned.1.call-start = ((), (), s32[]{:S(2)}) async-start(), calls=%async_computation.7 | async-start | bytes 1572864 | tf_op jit(solution)/shard_map/psum | solution.py:20
  469.2 135.1 %all-reduce.13.cloned.1.call-start = ((), (), s32[]{:S(2)}) async-start(), calls=%async_computation.8 | async-start | bytes 1572864 | tf_op jit(solution)/shard_map/psum | solution.py:20
Sparse Core Ops, SparseCore 0:
  10.4 69.7 all-gather.1
  83.5 82.8 all-reduce.6
  169.3 81.2 all-reduce.8
  332.3 94.3 reduce-scatter.1
  469.3 78.6 all-reduce.10
  550.7 53.5 all-reduce.12
where the time goes:
time: 621 us
  waiting for transfers between devices  494 us (80%)
  blocking collectives  54.5 us (9%)
  matrix products  16.5 us (3%)
  starting transfers between devices  15.4 us (2%)
  local copies, waits for them, and re-layouts  14.8 us (2%)
  between operations  13.6 us (2%)
  other arithmetic  11.7 us (2%)
    psum x4, waiting for transfers between devices, broadcast_by_axis(): value = lax.psum(value, axis)  299 us
    reduce_scatter x1, waiting for transfers between devices, spread(): own = lax.psum_scatter(padded, axis, scatter_dimension=0, tiled=True)  94.5 us
    all_gather x1, waiting for transfers between devices, shards(): rows_local = lax.all_gather(child_panel, 'col', axis=1, tiled=True)[0]  72.9 us
    all_gather x1, blocking collectives, spread(): lax.all_gather(own, axis, axis=0, tiled=True)[:len(lines)]  41.6 us
    ppermute x2, waiting for transfers between devices, shifted(): lax.ppermute(value, axis, [(source, source + steps) for source in range(i...  26.9 us
    ppermute x2, starting transfers between devices, shifted(): lax.ppermute(value, axis, [(source, source + steps) for source in range(i...  15.2 us
  transfers between devices with their start and end apart: 8, of which 8 were waited for; matrix products, arithmetic and copies ran while one was open for 1% of the time, Pallas kernels for 0%

commit v1 on v0

--- a/solution.py
+++ b/solution.py
@@ -17,7 +17,7 @@
 def broadcast_by_axis(value, axes, root):
     value = jnp.where(lax.axis_index(axes) == root, value, jnp.zeros_like(value))
     for axis in axes:
-        value = lax.psum(value, axis)
+        value = jnp.sum(lax.all_gather(value, axis), axis=0)
     return value
 
 

time: 621 us -> 689 us (1.11)
  waiting for transfers between devices: 494 us -> 543 us
  other arithmetic: 11.7 us -> 30.7 us
    all_gather x0 -> x4, waiting for transfers between devices: none -> 348 us  [broadcast_by_axis(): value = jnp.sum(lax.all_gather(value, axis), axis=0)]
    psum x4 -> x0, waiting for transfers between devices: 299 us -> none  [broadcast_by_axis(): value = lax.psum(value, axis)]
    reduce_sum x0 -> x4, other arithmetic: none -> 19 us  [broadcast_by_axis(): value = jnp.sum(lax.all_gather(value, axis), axis=0)]
  transfers between devices with their start and end apart: 8 -> 8, of which waited for: 8 -> 8; matrix products, arithmetic and copies ran while one was open for 1% -> 0% of each run, Pallas kernels for 0% -> 0%
where the time goes in v1:
time: 689 us; the launch traced here: 688 us
  waiting for transfers between devices  543 us (79%)
  blocking collectives  54.4 us (8%)
  other arithmetic  30.7 us (4%)
  matrix products  16.5 us (2%)
  starting transfers between devices  15.4 us (2%)
  local copies, waits for them, and re-layouts  14.6 us (2%)
  between operations  13.6 us (2%)
    all_gather x4, waiting for transfers between devices, broadcast_by_axis(): value = jnp.sum(lax.all_gather(value, axis), axis=0)  348 us
    reduce_scatter x1, waiting for transfers between devices, spread(): own = lax.psum_scatter(padded, axis, scatter_dimension=0, tiled=True)  94.6 us
    all_gather x1, waiting for transfers between devices, shards(): rows_local = lax.all_gather(child_panel, 'col', axis=1, tiled=True)[0]  72.9 us
    all_gather x1, blocking collectives, spread(): lax.all_gather(own, axis, axis=0, tiled=True)[:len(lines)]  41.5 us
    ppermute x2, waiting for transfers between devices, shifted(): lax.ppermute(value, axis, [(source, source + steps) for source in range(i...  26.9 us
    reduce_sum x4, other arithmetic, broadcast_by_axis(): value = jnp.sum(lax.all_gather(value, axis), axis=0)  19 us
    ppermute x2, starting transfers between devices, shifted(): lax.ppermute(value, axis, [(source, source + steps) for source in range(i...  15.2 us
  transfers between devices with their start and end apart: 8, of which 8 were waited for; matrix products, arithmetic and copies ran while one was open for 0% of the time, Pallas kernels for 0%

profile of v1, /device:TPU:1, one launch (start us, length us, event | category | flops | bytes accessed | tf_op | source)
XLA Modules:
  0.0 688.1 jit_solution(6151833570485412134)
XLA Ops:
  6.5 0.7 all-gather.9.cloned.1.call-update
  7.3 0.0 all-gather.11.cloned.1.call-start
  7.3 72.9 %all-gather.9.cloned.1.call-done = f32[1,512,1024]{2,1,0:T(8,128)} async-done(((f32[1,32,1024]{2,1,0:T(8,128)}), f32[1,512,1024]{2,1,0:T(8,128)}) %all-gather.9.cloned.1.call-update) | async-done | bytes 2097168 | tf_op jit(solution)/shard_map/all_gather | solution.py:100
  80.2 3.2 broadcast_select_fusion
  83.3 0.0 all-gather.11.cloned.1.call-update
  83.4 0.0 all-gather.13.cloned.1.call-start
  83.4 173.4 %all-gather.11.cloned.1.call-done = f32[8,512,1024]{2,1,0:T(8,128)} async-done(((f32[1,512,1024]{2,1,0:T(8,128)}), f32[8,512,1024]{2,1,0:T(8,128)}) %all-gather.11.cloned.1.call-update) | async-done | bytes 16777232 | tf_op jit(solution)/shard_map/all_gather | solution.py:20
  256.8 9.3 %reduce_sum.45 = f32[512,1024]{1,0:T(8,128)} reduce(f32[8,512,1024]{2,1,0:T(8,128)} %all-gather.11.cloned.1.call-done, f32[]{:T(128)} %constant.45.clone.1), dimensions={0}, to_apply=%region_0.1 | reduce | flops 3670016 | bytes 18874372 | tf_op jit(solution)/shard_map/reduce_sum | solution.py:20
  266.1 0.0 all-gather.13.cloned.1.call-update
  266.1 0.0 reduce-scatter.2.cloned.1.call-start
  266.1 1.1 copy-done.2
  267.3 1.3 copy.22
  268.6 60.4 %all-gather.13.cloned.1.call-done = f32[1024,1024]{1,0:T(8,128)} async-done(((f32[512,1024]{1,0:T(8,128)}), f32[1024,1024]{1,0:T(8,128)}) %all-gather.13.cloned.1.call-update) | async-done | bytes 4194320 | tf_op jit(solution)/shard_map/all_gather | solution.py:20
  329.0 2.8 reduce_sum.46
  331.8 5.4 fusion.8
  337.2 1.0 copy-done.1
  338.2 4.1 collective-permute-start
  342.3 0.1 pad_dynamic-slice_fusion.1
  342.4 13.7 %collective-permute-done = f32[512,256]{0,1:T(8,128)S(1)} collective-permute-done((f32[512,256]{0,1:T(8,128)S(1)}, f32[512,256]{0,1:T(8,128)S(1)}, u32[]{:S(2)}, u32[]{:S(2)}) %collective-permute-start) | collective-permute-done | bytes 524320 | tf_op jit(solution)/shard_map/ppermute | solution.py:27
  356.2 1.3 pad_maximum_fusion.1
  357.5 1.8 copy.23
  359.4 2.7 convolution_bitcast_fusion
  362.0 1.0 slice.17
  363.1 2.4 copy.24
  365.5 11.1 %collective-permute-start.1 = (f32[256,768]{0,1:T(8,128)}, f32[256,768]{0,1:T(8,128)}, u32[]{:S(2)}, u32[]{:S(2)}) collective-permute-start(f32[256,768]{0,1:T(8,128)} %bitcast.45), channel_id=1, source_target_pairs={{0,16},{16,32},{32,48},{48,64},{64,80},{80,96},{96,112},{112,128},... | collective-permute-start | bytes 2359304 | tf_op jit(solution)/shard_map/ppermute | solution.py:27
  376.6 1.6 copy.25
  378.2 13.2 %collective-permute-done.1 = f32[256,768]{0,1:T(8,128)} collective-permute-done((f32[256,768]{0,1:T(8,128)}, f32[256,768]{0,1:T(8,128)}, u32[]{:S(2)}, u32[]{:S(2)}) %collective-permute-start.1) | collective-permute-done | bytes 786464 | tf_op jit(solution)/shard_map/ppermute | solution.py:27
  391.4 3.2 pad_maximum_fusion
  394.6 2.0 copy.26
  396.6 2.9 fusion
  399.5 0.8 copy.28
  400.3 7.6 %all_to_all.10 = f32[2,384,768]{2,1,0:T(8,128)S(1)} all-to-all(f32[2,384,768]{2,1,0:T(8,128)S(1)} %bitcast.38), channel_id=1, replica_groups=mesh['sib'=2,'row_0'=8,'row_1'=2,'col'=16] {'sib'}, dimensions={0} | all-to-all | bytes 4718592 | tf_op jit(solution)/shard_map/all_to_all | solution.py:38
  407.9 1.3 reduce_sum.47
  409.2 1.8 add.80
  410.9 2.3 convolution_select_fusion
  413.3 0.0 reduce-scatter.2.cloned.1.call-update
  413.3 0.0 all-gather.15.cloned.1.call-start
  413.3 94.6 %reduce-scatter.2.cloned.1.call-done = f32[24,512]{1,0:T(8,128)} async-done(((f32[384,512]{1,0:T(8,128)}), f32[24,512]{1,0:T(8,128)}) %reduce-scatter.2.cloned.1.call-update) | async-done | bytes 49168 | tf_op jit(solution)/shard_map/reduce_scatter | solution.py:52
  507.9 41.5 %all_gather.32 = f32[384,512]{1,0:T(8,128)S(1)} all-gather(f32[24,512]{1,0:T(8,128)} %reduce-scatter.2.cloned.1.call-done), channel_id=1, replica_groups=mesh['sib'=2,'row_0'=8,'row_1'=2,'col'=16] {'col'}, dimensions={0}, use_global_device_ids=true | all-gather | bytes 835584 | tf_op jit(solution)/shard_map/all_gather | solution.py:53
  549.4 0.9 broadcast_select_fusion.1
  550.4 0.0 all-gather.17.cloned.1.call-start
  550.5 80.7 %all-gather.15.cloned.1.call-done = f32[3072,512]{1,0:T(8,128)} async-done(((f32[384,512]{1,0:T(8,128)}), f32[3072,512]{1,0:T(8,128)}) %all-gather.15.cloned.1.call-update) | async-done | bytes 6291472 | tf_op jit(solution)/shard_map/all_gather | solution.py:20
  631.1 4.5 reduce_sum.48
  635.7 33.3 %all-gather.17.cloned.1.call-done = f32[768,512]{1,0:T(8,128)} async-done(((f32[384,512]{1,0:T(8,128)}), f32[768,512]{1,0:T(8,128)}) %all-gather.17.cloned.1.call-update) | async-done | bytes 1572880 | tf_op jit(solution)/shard_map/all_gather | solution.py:20
  668.9 2.5 reduce_sum.49
  671.4 1.3 broadcast_in_dim.11
  672.8 5.3 all_to_all.11
  678.1 3.2 fusion.4
  (15 shorter events, 0.1 us)
Async XLA Ops:
  6.5 404.4 %copy-start = (f32[512,512]{1,0:T(8,128)S(1)}, f32[512,512]{1,0:T(8,128)}, u32[]{:S(2)}) copy-start(f32[512,512]{1,0:T(8,128)} %param.9) | copy-start | bytes 3145732
  6.5 73.6 %all-gather.9.cloned.1.call-start = ((), (), s32[]{:S(2)}) async-start(), calls=%async_computation.3 | async-start | bytes 2228224 | tf_op jit(solution)/shard_map/all_gather | solution.py:100
  7.3 249.5 %all-gather.11.cloned.1.call-start = ((), (), s32[]{:S(2)}) async-start(), calls=%async_computation.4 | async-start | bytes 18874368 | tf_op jit(solution)/shard_map/all_gather | solution.py:20
  83.4 245.6 %all-gather.13.cloned.1.call-start = ((), (), s32[]{:S(2)}) async-start(), calls=%async_computation.6 | async-start | bytes 6291456 | tf_op jit(solution)/shard_map/all_gather | solution.py:20
  266.1 1.2 copy-start.2
  266.1 241.8 %reduce-scatter.2.cloned.1.call-start = ((), (), s32[]{:S(2)}) async-start(), calls=%async_computation.5 | async-start | bytes 835584 | tf_op jit(solution)/shard_map/reduce_scatter | solution.py:52
  331.8 10.5 %copy-start.3 = (s32[2,64]{1,0:T(2,128)S(1)}, s32[2,64]{1,0:T(2,128)}, u32[]{:S(2)}) copy-start(s32[2,64]{1,0:T(2,128)} %param.7) | copy-start | bytes 1540
  337.2 1.0 copy-start.1
  338.2 17.9 %collective-permute-start = (f32[512,256]{0,1:T(8,128)S(1)}, f32[512,256]{0,1:T(8,128)S(1)}, u32[]{:S(2)}, u32[]{:S(2)}) collective-permute-start(f32[512,256]{0,1:T(8,128)S(1)} %slice.16), channel_id=1, source_target_pairs={{0,1},{1,2},{2,3},{3,4},{4,5},{5,6},{6,7},{7,8},{8,9},{9,10},{10,1... | collective-permute-start | bytes 1572872 | tf_op jit(solution)/shard_map/ppermute | solution.py:27
  365.5 25.9 %collective-permute-start.1 = (f32[256,768]{0,1:T(8,128)}, f32[256,768]{0,1:T(8,128)}, u32[]{:S(2)}, u32[]{:S(2)}) collective-permute-start(f32[256,768]{0,1:T(8,128)} %bitcast.45), channel_id=1, source_target_pairs={{0,16},{16,32},{32,48},{48,64},{64,80},{80,96},{96,112},{112,128},... | collective-permute-start | bytes 2359304 | tf_op jit(solution)/shard_map/ppermute | solution.py:27
  413.3 217.8 %all-gather.15.cloned.1.call-start = ((), (), s32[]{:S(2)}) async-start(), calls=%async_computation.7 | async-start | bytes 7077888 | tf_op jit(solution)/shard_map/all_gather | solution.py:20
  550.4 118.5 %all-gather.17.cloned.1.call-start = ((), (), s32[]{:S(2)}) async-start(), calls=%async_computation.8 | async-start | bytes 2359296 | tf_op jit(solution)/shard_map/all_gather | solution.py:20
Sparse Core Ops, SparseCore 0:
  10.4 69.7 all-gather.8
  83.5 173.2 all-gather.10
  266.2 62.7 all-gather.12
  413.4 94.4 reduce-scatter.1
  550.5 80.5 all-gather.14
  635.7 33.1 all-gather.16
